TPU v7x, 32 devices: a whole 2x2x4 slice. The times are simulated.
32 devices in a mesh: tp: 8 (over y, x, core), grp: 4 (over z).
Axes of the slice: x: 2, y: 2, z: 4, core: 2. Of those that a mesh axis runs over, the one named last changes fastest.
Arguments:
- resid_in: bfloat16 [256, 8192], P('grp', 'tp'), may hold values from -6 to 6
- queries: bfloat16 [256, 4096], P('grp', 'tp')
- kv_cache: bfloat16 [2, 256, 8, 128, 128], P(None, 'grp', 'tp'), as said below
- new_kv: bfloat16 [2, 256, 4, 128], P(None, 'grp')
- lengths: int32 [256], P('grp'), may hold values from 1 to 128, 16384 in all
- out_weight: bfloat16 [4096, 8192], P('tp'), may hold values from -0.09375 to 0.09375
- enc_weight: bfloat16 [8192, 32768], P('tp', 'grp'), may hold values from -0.0625 to 0.0625
- enc_bias: float32 [32768], P('grp'), may hold values from -1 to 0.5
- dec_weight: bfloat16 [32768, 8192], P('grp', 'tp'), may hold values from -0.75 to 0.75
- clamp_ids: int32 [256, 4], P('grp'), may hold values from 0 to 32767, as said below
- clamp_values: float32 [256, 4], P('grp'), may hold values from 2 to 8
Outputs:
- resid_out: bfloat16 [256, 8192], P('grp', 'tp')
- features: bfloat16 [256, 32768], P('tp', 'grp')
Inputs may be any that keep to these rules, and one draw needn't show every extreme that they name: Entries of kv_cache whose third index divided by 2 agrees are equal. `clamp_ids`: a row's 4 ids are (b + c * 8192) modulo 32768 for c = 0 .. 3.
All inputs are finite; a program needn't handle non-finite values. No bound on the sum of `lengths` on one device may be relied on, other than what follows from the above.
Results may differ from a plain program's by a relative error of at most 0.008.
Values may be sent and summed in bfloat16 or wider, within the bound.
A program may use at most 128 MiB of HBM per device.

v0:
```python
import jax
import jax.numpy as jnp
from jax import lax
from jax.sharding import PartitionSpec as P

HEAD_DIM = 128
KV_HEADS = 4


def clamp_delta(latent_block, id_table, value_table, offset):
    width = latent_block.shape[1]
    columns = jnp.arange(width, dtype=jnp.int32)
    local_ids = id_table - offset
    current = latent_block.astype(jnp.float32)
    delta_total = jnp.zeros(latent_block.shape, jnp.float32)
    for slot_index in range(id_table.shape[1]):
        is_hit = columns[None, :] == local_ids[:, slot_index : slot_index + 1]
        clamped_now = jnp.sum(jnp.where(is_hit, current, 0.0), axis=1, keepdims=True)
        delta_total = delta_total + jnp.where(
            is_hit, value_table[:, slot_index : slot_index + 1] - clamped_now, 0.0
        )
    return delta_total.astype(jnp.bfloat16)


def per_device(
    resid_in,
    queries,
    kv_cache,
    new_kv,
    lengths,
    out_weight,
    enc_weight,
    enc_bias,
    dec_weight,
    clamp_ids,
    clamp_values,
):
    tp_count = lax.axis_size("tp")
    tp_rank = lax.axis_index("tp")
    grp_rank = lax.axis_index("grp")
    row_count = resid_in.shape[0]
    own_heads = queries.shape[1] // HEAD_DIM
    slot_count = kv_cache.shape[3]
    score_scale = HEAD_DIM ** (-0.5)
    query_heads = queries.reshape(row_count, own_heads, HEAD_DIM)
    cache_keys = kv_cache[0, :, 0]
    cache_values = kv_cache[1, :, 0]
    kv_index = tp_rank // (tp_count // KV_HEADS)
    new_key = lax.dynamic_index_in_dim(new_kv[0], kv_index, 1, keepdims=False)
    new_value = lax.dynamic_index_in_dim(new_kv[1], kv_index, 1, keepdims=False)
    scores = (
        jnp.einsum("shd,spd->shp", query_heads, cache_keys, preferred_element_type=jnp.float32)
        * score_scale
    )
    new_score = (
        jnp.einsum("shd,sd->sh", query_heads, new_key, preferred_element_type=jnp.float32)
        * score_scale
    )
    slot_index = jnp.arange(slot_count, dtype=jnp.int32)
    is_valid = (slot_index[None, :] < lengths[:, None])[:, None, :]
    top_score = jnp.maximum(jnp.max(jnp.where(is_valid, scores, -jnp.inf), axis=-1), new_score)
    prob_cache = jnp.where(is_valid, jnp.exp(scores - top_score[..., None]), 0.0)
    new_prob = jnp.exp(new_score - top_score)
    total_weight = jnp.sum(prob_cache, axis=-1) + new_prob
    new_rounded = lax.optimization_barrier(new_prob.astype(jnp.bfloat16)).astype(jnp.float32)
    weighted = jnp.einsum(
        "shp,spd->shd",
        prob_cache.astype(jnp.bfloat16),
        cache_values,
        preferred_element_type=jnp.float32,
    )
    weighted = weighted + new_rounded[..., None] * new_value.astype(jnp.float32)[:, None, :]
    head_output = (
        (weighted / total_weight[..., None])
        .astype(jnp.bfloat16)
        .reshape(row_count, own_heads * HEAD_DIM)
    )
    attn_part = jnp.dot(head_output, out_weight, preferred_element_type=jnp.float32)
    attn_cols = lax.psum_scatter(attn_part, "tp", scatter_dimension=1, tiled=True)
    resid_mid = (resid_in.astype(jnp.float32) + attn_cols).astype(jnp.bfloat16)
    id_table, value_table = (
        lax.all_gather(clamp_ids, "grp", axis=0, tiled=True),
        lax.all_gather(clamp_values, "grp", axis=0, tiled=True),
    )
    pre_part = jnp.dot(
        lax.all_gather(resid_mid, "grp", axis=0, tiled=True),
        enc_weight,
        preferred_element_type=jnp.float32,
    )
    all_rows = pre_part.shape[0]
    lat_span = enc_weight.shape[1]
    span_start = grp_rank * lat_span
    pre_act = lax.psum(pre_part, "tp")
    latent_block = jnp.maximum(pre_act + enc_bias, 0.0).astype(jnp.bfloat16)
    out_rows = all_rows // tp_count
    feature_out = lax.dynamic_slice_in_dim(latent_block, tp_rank * out_rows, out_rows, 0)
    delta_lat = clamp_delta(latent_block, id_table, value_table, span_start)
    edit_part = jnp.dot(delta_lat, dec_weight, preferred_element_type=jnp.float32)
    edit_whole = lax.psum(edit_part, "grp")
    edit_mine = lax.dynamic_slice_in_dim(edit_whole, grp_rank * row_count, row_count, 0)
    resid_out = (resid_mid.astype(jnp.float32) + edit_mine).astype(jnp.bfloat16)
    return (resid_out, feature_out)


def solution(mesh):
    placed = (
        P("grp", "tp"),
        P("grp", "tp"),
        P(None, "grp", "tp", None, None),
        P(None, "grp", None, None),
        P("grp"),
        P("tp", None),
        P("tp", "grp"),
        P("grp"),
        P("grp", "tp"),
        P("grp", None),
        P("grp", None),
    )
    return jax.shard_map(
        per_device,
        mesh=mesh,
        in_specs=placed,
        out_specs=(P("grp", "tp"), P("tp", "grp")),
        check_vma=False,
    )
```

profile of v0, /device:TPU:0, one launch (start us, length us, event | category | flops | bytes accessed | tf_op | source)
XLA Modules:
  0.0 306.2 jit_solution(11197945177065684465)
XLA Ops:
  7.2 0.0 reduce-scatter.2.cloned.1.call-start
  7.2 0.9 fusion.35
  8.2 0.1 dynamic-slice_convert_fusion
  8.2 0.9 reshape.42
  9.1 0.7 iota_compare_fusion.4
  9.8 0.2 fusion.29
  10.0 2.9 select_reduce_fusion
  12.9 0.2 fusion.20
  13.2 2.3 fusion.19
  15.5 0.0 copy-start
  15.5 6.3 %fusion.23 = f32[64,8192]{1,0:T(8,128)} fusion(bf16[512,8192]{1,0:T(8,128)(2,1)} %param.16, bf16[8,8,4,128]{3,2,1,0:T(4,128)(2,1)S(1)} %bitcast.56), kind=kOutput, calls=%fused_computation.38 | convolution fusion | flops 536870912 | bytes 10551296 | tf_op jit(solution)/shard_map/dot_general | solution.py:78
  21.9 0.0 reduce-scatter.2.cloned.1.call-update
  21.9 0.0 all-reduce.3.cloned.1.call-start
  21.9 44.0 %reduce-scatter.2.cloned.1.call-done = f32[64,1024]{1,0:T(8,128)} async-done(((f32[64,8192]{1,0:T(8,128)}), f32[64,1024]{1,0:T(8,128)}) %reduce-scatter.2.cloned.1.call-update) | async-done | bytes 262160 | tf_op jit(solution)/shard_map/reduce_scatter | solution.py:79
  65.9 0.0 copy-done
  66.0 1.0 add_convert_fusion.3
  66.9 15.6 %all_gather.11 = bf16[256,1024]{1,0:T(8,128)(2,1)S(1)} all-gather(bf16[64,1024]{1,0:T(8,128)(2,1)S(1)} %add_convert_fusion.3), channel_id=1, replica_groups=mesh['tp'=8,'grp'=4] {'grp'}, dimensions={0}, use_global_device_ids=true | all-gather | bytes 655360 | tf_op jit(solution)/shard_map/all_gather | solution.py:86
  82.6 12.4 %fusion.37 = f32[256,8192]{1,0:T(8,128)} fusion(bf16[256,1024]{1,0:T(8,128)(2,1)S(1)} %all_gather.11, bf16[1024,8192]{1,0:T(8,128)(2,1)} %param.17), kind=kOutput, calls=%fused_computation.64 | convolution fusion | flops 4294967296 | bytes 25690112 | tf_op jit(solution)/shard_map/dot_general | solution.py:85
  95.0 0.0 copy-start.2
  95.0 0.0 copy-start.3
  95.0 0.0 copy-start.1
  95.0 0.0 all-reduce.3.cloned.1.call-update
  95.1 0.0 all-reduce.5.cloned.1.call-start
  95.1 0.6 copy-done.2
  95.7 12.2 %all-gather = s32[4,64,4]{1,2,0:T(4,128)S(1)} all-gather(s32[1,64,4]{1,2,0:T(4,128)S(1)} %bitcast.75), channel_id=1, replica_groups=mesh['tp'=8,'grp'=4] {'grp'}, dimensions={0}, use_global_device_ids=true | all-gather | bytes 5120 | tf_op jit(solution)/shard_map/all_gather | solution.py:82
  107.9 0.1 reshape.50
  108.0 0.0 copy-done.3
  108.0 12.0 %all-gather.1 = f32[4,64,4]{1,2,0:T(4,128)S(1)} all-gather(f32[1,64,4]{1,2,0:T(4,128)S(1)} %bitcast.76), channel_id=1, replica_groups=mesh['tp'=8,'grp'=4] {'grp'}, dimensions={0}, use_global_device_ids=true | all-gather | bytes 5120 | tf_op jit(solution)/shard_map/all_gather | solution.py:83
  120.0 0.1 reshape.48
  120.1 102.5 %all-reduce.3.cloned.1.call-done = f32[256,8192]{1,0:T(8,128)} async-done(((f32[256,8192]{1,0:T(8,128)}), f32[256,8192]{1,0:T(8,128)}) %all-reduce.3.cloned.1.call-update) | async-done | bytes 8388624 | tf_op jit(solution)/shard_map/psum | solution.py:93
  222.6 0.0 copy-done.1
  222.6 9.3 %fusion = (f32[256]{0:T(256)S(1)}, f32[256]{0:T(256)S(1)}, f32[256]{0:T(256)S(1)}, f32[256]{0:T(256)S(1)}, bf16[256,8192]{1,0:T(8,128)(2,1)}) fusion(s32[256]{0:T(256)S(1)} %bitcast.73, s32[256]{0:T(256)S(1)} %bitcast.71, s32[256]{0:T(256)S(1)} %bitcast.69, s32[256]{0:T(256)S(1)} %bitcast.67, f32[256,8192]{1,0:T(8,128)} %all-reduce.3.cloned.1.call-done, ...), kind=kLoop, calls=%fused_computation.4 | loop fusion | flops 33553408 | bytes 12623872 | tf_op jit(solution)/shard_map/reduce_sum | solution.py:18
  231.9 14.0 %fusion.4 = f32[256,1024]{1,0:T(8,128)} fusion(bf16[8192,1024]{1,0:T(8,128)(2,1)} %param.19, f32[256]{0:T(256)S(1)} %bitcast.78, s32[256]{0:T(256)S(1)} %bitcast.68, f32[256]{0:T(256)S(1)} %bitcast.79, s32[256]{0:T(256)S(1)} %bitcast.70, f32[256]{0:T(256)S(1)} %bitcast.80, s32[256]{0:T(256)S(1)} %bitcast.72, f32[256]{0:T(256)S(1)} %bitcast.77, ...), kind=kOutput, calls=%fused_computation.14 | convolution fusion | flops 4320133120 | bytes 17833984 | tf_op jit(solution)/shard_map/dot_general | solution.py:98
  245.9 0.0 all-reduce.5.cloned.1.call-update
  245.9 1.9 constant_dynamic-slice_fusion
  247.8 50.3 %all-reduce.5.cloned.1.call-done = f32[256,1024]{1,0:T(8,128)} async-done(((f32[256,1024]{1,0:T(8,128)}), f32[256,1024]{1,0:T(8,128)}) %all-reduce.5.cloned.1.call-update) | async-done | bytes 1048592 | tf_op jit(solution)/shard_map/psum | solution.py:99
  298.1 1.6 add_convert_fusion.2
  (9 shorter events, 0.1 us)
Async XLA Ops:
  7.2 58.8 %reduce-scatter.2.cloned.1.call-start = ((), (), s32[]{:S(2)}) async-start(), calls=%async_computation.1 | async-start | bytes 2359296 | tf_op jit(solution)/shard_map/reduce_scatter | solution.py:79
  15.5 50.4 %copy-start = (bf16[64,1024]{1,0:T(8,128)(2,1)S(1)}, bf16[64,1024]{1,0:T(8,128)(2,1)}, u32[]{:S(2)}) copy-start(bf16[64,1024]{1,0:T(8,128)(2,1)} %param.11) | copy-start | bytes 393220
  21.9 200.7 %all-reduce.3.cloned.1.call-start = ((), (), s32[]{:S(2)}) async-start(), calls=%async_computation.2 | async-start | bytes 16777216 | tf_op jit(solution)/shard_map/psum | solution.py:93
  95.0 0.7 copy-start.2
  95.0 12.9 %copy-start.3 = (f32[64,4]{0,1:T(4,128)S(1)}, f32[64,4]{0,1:T(4,128)}, u32[]{:S(2)}) copy-start(f32[64,4]{0,1:T(4,128)} %param.21) | copy-start | bytes 3076
  95.0 127.6 %copy-start.1 = (f32[8192]{0:T(1024)S(1)}, f32[8192]{0:T(1024)}, u32[]{:S(2)}) copy-start(f32[8192]{0:T(1024)} %param.18) | copy-start | bytes 98308
  95.1 203.0 %all-reduce.5.cloned.1.call-start = ((), (), s32[]{:S(2)}) async-start(), calls=%async_computation.3 | async-start | bytes 2097152 | tf_op jit(solution)/shard_map/psum | solution.py:99
Sparse Core Ops, SparseCore 0:
  22.0 43.8 reduce-scatter.1
  95.2 127.3 all-reduce.2
  246.0 51.9 all-reduce.4
where the time goes:
time: 307 us; the launch traced here: 306 us
  waiting for transfers between devices  197 us (64%)
  blocking collectives  39.9 us (13%)
  matrix products  38.1 us (12%)
  between operations  13.8 us (4%)
  other arithmetic  13 us (4%)
  local copies, waits for them, and re-layouts  4.46 us (1%)
    psum x1, waiting for transfers between devices, per_device(): pre_act = lax.psum(pre_part, 'tp')  102 us
    psum x1, waiting for transfers between devices, per_device(): edit_whole = lax.psum(edit_part, 'grp')  50.3 us
    reduce_scatter x1, waiting for transfers between devices, per_device(): lax.psum_scatter(attn_part, 'tp', scatter_dimension=1, tiled=True)  44 us
    all_gather x1, blocking collectives, per_device(): lax.all_gather(resid_mid, 'grp', axis=0, tiled=True)  15.6 us
    dot_general x1, matrix products, per_device(): jnp.dot(delta_lat, dec_weight, preferred_element_type=jnp.float32)  14 us
    dot_general x1, matrix products, per_device(): jnp.dot(lax.all_gather(resid_mid, 'grp', axis=0, tiled=True), enc_weight,...  12.4 us
    all_gather x1, blocking collectives, per_device(): lax.all_gather(clamp_ids, 'grp', axis=0, tiled=True)  12.2 us
    all_gather x1, blocking collectives, per_device(): lax.all_gather(clamp_values, 'grp', axis=0, tiled=True)  12 us
  transfers between devices with their start and end apart: 3, of which 3 were waited for; matrix products, arithmetic and copies ran while one was open for 1% of the time, Pallas kernels for 0%

commit v1 on v0

--- a/solution.py
+++ b/solution.py
@@ -5,21 +5,6 @@
 
 HEAD_DIM = 128
 KV_HEADS = 4
-
-
-def clamp_delta(latent_block, id_table, value_table, offset):
-    width = latent_block.shape[1]
-    columns = jnp.arange(width, dtype=jnp.int32)
-    local_ids = id_table - offset
-    current = latent_block.astype(jnp.float32)
-    delta_total = jnp.zeros(latent_block.shape, jnp.float32)
-    for slot_index in range(id_table.shape[1]):
-        is_hit = columns[None, :] == local_ids[:, slot_index : slot_index + 1]
-        clamped_now = jnp.sum(jnp.where(is_hit, current, 0.0), axis=1, keepdims=True)
-        delta_total = delta_total + jnp.where(
-            is_hit, value_table[:, slot_index : slot_index + 1] - clamped_now, 0.0
-        )
-    return delta_total.astype(jnp.bfloat16)
 
 
 def per_device(
@@ -76,28 +61,40 @@
         .reshape(row_count, own_heads * HEAD_DIM)
     )
     attn_part = jnp.dot(head_output, out_weight, preferred_element_type=jnp.float32)
-    attn_cols = lax.psum_scatter(attn_part, "tp", scatter_dimension=1, tiled=True)
+    attn_cols = lax.psum_scatter(
+        attn_part.astype(jnp.bfloat16), "tp", scatter_dimension=1, tiled=True
+    ).astype(jnp.float32)
     resid_mid = (resid_in.astype(jnp.float32) + attn_cols).astype(jnp.bfloat16)
-    id_table, value_table = (
-        lax.all_gather(clamp_ids, "grp", axis=0, tiled=True),
-        lax.all_gather(clamp_values, "grp", axis=0, tiled=True),
+    table = lax.all_gather(
+        jnp.concatenate([clamp_ids.astype(jnp.float32), clamp_values], axis=1),
+        "grp", axis=0, tiled=True,
     )
+    slots = clamp_ids.shape[1]
+    lat_span = enc_weight.shape[1]
+    local = table[:, :slots].astype(jnp.int32) - grp_rank * lat_span
+    inside = (local >= 0) & (local < lat_span)
+    hit_any = jnp.any(inside, axis=1)
+    local_id = jnp.sum(jnp.where(inside, local, 0), axis=1)
+    target = jnp.sum(jnp.where(inside, table[:, slots:], 0.0), axis=1)
     pre_part = jnp.dot(
         lax.all_gather(resid_mid, "grp", axis=0, tiled=True),
         enc_weight,
         preferred_element_type=jnp.float32,
     )
-    all_rows = pre_part.shape[0]
-    lat_span = enc_weight.shape[1]
-    span_start = grp_rank * lat_span
-    pre_act = lax.psum(pre_part, "tp")
-    latent_block = jnp.maximum(pre_act + enc_bias, 0.0).astype(jnp.bfloat16)
-    out_rows = all_rows // tp_count
-    feature_out = lax.dynamic_slice_in_dim(latent_block, tp_rank * out_rows, out_rows, 0)
-    delta_lat = clamp_delta(latent_block, id_table, value_table, span_start)
-    edit_part = jnp.dot(delta_lat, dec_weight, preferred_element_type=jnp.float32)
-    edit_whole = lax.psum(edit_part, "grp")
-    edit_mine = lax.dynamic_slice_in_dim(edit_whole, grp_rank * row_count, row_count, 0)
+    columns = jnp.arange(lat_span, dtype=jnp.int32)
+    is_hit = columns[None, :] == local_id[:, None]
+    picked = lax.psum(jnp.sum(jnp.where(is_hit, pre_part, 0.0), axis=1), "tp")
+    pre_act = lax.psum_scatter(
+        pre_part.astype(jnp.bfloat16), "tp", scatter_dimension=0, tiled=True
+    ).astype(jnp.float32)
+    feature_out = jnp.maximum(pre_act + enc_bias, 0.0).astype(jnp.bfloat16)
+    current = jnp.maximum(picked + enc_bias[local_id], 0.0).astype(jnp.bfloat16)
+    delta = (target - current.astype(jnp.float32)).astype(jnp.bfloat16).astype(jnp.float32)
+    delta = jnp.where(hit_any, delta, 0.0)
+    edit_part = delta[:, None] * dec_weight[local_id].astype(jnp.float32)
+    edit_mine = lax.psum_scatter(
+        edit_part.astype(jnp.bfloat16), "grp", scatter_dimension=0, tiled=True
+    ).astype(jnp.float32)
     resid_out = (resid_mid.astype(jnp.float32) + edit_mine).astype(jnp.bfloat16)
     return (resid_out, feature_out)
 

time: 307 us -> 187 us (0.61)
  waiting for transfers between devices: 197 us -> 86.5 us
  matrix products: 38.1 us -> 23.5 us
  local copies, waits for them, and re-layouts: 4.46 us -> 13.1 us
  other arithmetic: 13 us -> 6.61 us
    psum x2 -> x0, waiting for transfers between devices: 153 us -> none  [the longest x1 102 us: per_device(): pre_act = lax.psum(pre_part, 'tp')]
    reduce_scatter x1 -> x3, waiting for transfers between devices: 44 us -> 85.8 us  [the longest x1 51.4 us: per_device(): lax.psum_scatter(pre_part.astype(jnp.bfloat16), 'tp', scatter_dimension=0...]
    dot_general x1 -> x0, matrix products: 14 us -> none  [per_device(): jnp.dot(delta_lat, dec_weight, preferred_element_type=jnp.float32)]
    psum x0 -> x1, blocking collectives: none -> 11.8 us  [per_device(): picked = lax.psum(jnp.sum(jnp.where(is_hit, pre_part, 0.0), axis=1), 'tp')]
    gather x0 -> x2, local copies, waits for them, and re-layouts: none -> 11.2 us  [the longest x1 9.48 us: per_device(): edit_part = delta[:, None] * dec_weight[local_id].astype(jnp.float32)]
    all_gather x2 -> x1, blocking collectives: 24.2 us -> 14.8 us  [per_device(): lax.all_gather(jnp.concatenate([clamp_ids.astype(jnp.float32), clamp_valu...]
    reduce_sum x1 -> x2, other arithmetic: 9.31 us -> 0.05 us  [the longest x1 0.03 us: per_device(): target = jnp.sum(jnp.where(inside, table[:, slots:], 0.0), axis=1)]
  transfers between devices with their start and end apart: 3 -> 3, of which waited for: 3 -> 3; matrix products, arithmetic and copies ran while one was open for 1% -> 7% of each run, Pallas kernels for 0% -> 0%
where the time goes in v1:
time: 187 us; the launch traced here: 186 us
  waiting for transfers between devices  86.5 us (46%)
  blocking collectives  42.2 us (23%)
  matrix products  23.5 us (13%)
  between operations  13.9 us (7%)
  local copies, waits for them, and re-layouts  13.1 us (7%)
  other arithmetic  6.61 us (4%)
    reduce_scatter x1, waiting for transfers between devices, per_device(): lax.psum_scatter(pre_part.astype(jnp.bfloat16), 'tp', scatter_dimension=0...  51.4 us
    reduce_scatter x1, waiting for transfers between devices, per_device(): lax.psum_scatter(edit_part.astype(jnp.bfloat16), 'grp', scatter_dimension...  21.8 us
    all_gather x1, blocking collectives, per_device(): lax.all_gather(resid_mid, 'grp', axis=0, tiled=True)  15.6 us
    all_gather x1, blocking collectives, per_device(): lax.all_gather(jnp.concatenate([clamp_ids.astype(jnp.float32), clamp_valu...  14.8 us
    reduce_scatter x1, waiting for transfers between devices, per_device(): lax.psum_scatter(attn_part.astype(jnp.bfloat16), 'tp', scatter_dimension=...  12.6 us
    dot_general x1, matrix products, per_device(): jnp.dot(lax.all_gather(resid_mid, 'grp', axis=0, tiled=True), enc_weight,...  12.2 us
    psum x1, blocking collectives, per_device(): picked = lax.psum(jnp.sum(jnp.where(is_hit, pre_part, 0.0), axis=1), 'tp')  11.8 us
    gather x1, local copies, waits for them, and re-layouts, per_device(): edit_part = delta[:, None] * dec_weight[local_id].astype(jnp.float32)  9.48 us
  transfers between devices with their start and end apart: 3, of which 3 were waited for; matrix products, arithmetic and copies ran while one was open for 7% of the time, Pallas kernels for 0%

profile of v1, /device:TPU:0, one launch (start us, length us, event | category | flops | bytes accessed | tf_op | source)
XLA Modules:
  0.0 186.0 jit_solution(2356907583197260513)
XLA Ops:
  7.2 0.0 reduce-scatter.4.cloned.1.call-start
  7.2 0.9 fusion.22
  8.2 0.1 dynamic-slice_convert_fusion
  8.2 0.9 reshape.57
  9.1 0.7 iota_compare_fusion.1
  9.8 0.2 fusion.14
  10.0 2.9 %select_reduce_fusion.1 = (f32[64,4]{1,0:T(8,128)S(1)}, f32[64,4,128]{2,1,0:T(4,128)S(1)}) fusion(pred[64,128]{1,0:T(8,128)(4,1)S(1)} %iota_compare_fusion.1, bf16[64,4,128]{2,1,0:T(4,128)(2,1)S(1)} %reshape.57, bf16[2,64,1,128,128]{4,3,1,2,0:T(8,128)(2,1)} %bitcast.48), kind=kOutput, calls=%fused_computation.18 | convolution fusion | flops 8486656 | bytes 2302976 | tf_op jit(solution)/shard_map/shd,spd->shp/dot_general | solution.py:37
  12.9 0.2 fusion.6
  13.2 0.0 copy-start.2
  13.2 0.0 copy-start.3
  13.2 0.0 copy-start
  13.2 2.3 %fusion.5 = bf16[64,4,128]{2,1,0:T(4,128)(2,1)S(1)} fusion(bf16[2,64,1,128,128]{4,3,1,2,0:T(8,128)(2,1)} %bitcast.49, f32[64,4,128]{2,1,0:T(4,128)S(1)} %get-tuple-element.11, f32[64,4]{1,0:T(8,128)S(1)} %get-tuple-element.9, f32[64,128]{1,0:T(8,128)S(1)} %bitcast.44, f32[64,4]{1,0:T(8,128)S(1)} %convert_element_type.79, ...), kind=kOutput, calls=%fused_computation.12 | convolution fusion | flops 8617984 | bytes 2337792 | tf_op jit(solution)/shard_map/shp,spd->shd/dot_general | solution.py:51
  15.6 0.0 copy-start.1
  15.6 6.0 %convolution_convert_fusion = bf16[64,8192]{1,0:T(8,128)(2,1)} fusion(bf16[512,8192]{1,0:T(8,128)(2,1)} %param.16, bf16[8,8,4,128]{3,2,1,0:T(4,128)(2,1)S(1)} %bitcast.41), kind=kOutput, calls=%fused_computation.2 | convolution fusion | flops 537395200 | bytes 9502720 | tf_op jit(solution)/shard_map/dot_general | solution.py:63
  21.5 0.0 reduce-scatter.4.cloned.1.call-update
  21.6 0.0 reduce-scatter.6.cloned.1.call-start
  21.6 0.0 copy-done.2
  21.6 0.0 copy-done.3
  21.7 14.8 %all-gather = f32[4,64,8]{1,2,0:T(8,128)S(1)} all-gather(f32[1,64,8]{1,2,0:T(8,128)S(1)} %maximum_bitcast_fusion), channel_id=1, replica_groups=mesh['tp'=8,'grp'=4] {'grp'}, dimensions={0}, use_global_device_ids=true | all-gather | bytes 10240 | tf_op jit(solution)/shard_map/all_gather | solution.py:68
  36.5 0.1 reshape.77
  36.7 0.0 copy-done
  36.7 1.7 gather_fusion
  38.4 9.5 %gather_fusion.1 = bf16[256,1024]{1,0:T(8,128)(2,1)S(1)} fusion(bf16[8192,1024]{1,0:T(8,128)(2,1)} %param.19, s32[1024]{0:T(1024)S(1)} %pad_clamp_fusion), kind=kCustom, calls=%fused_computation.1 | custom fusion | bytes 1049600 | tf_op jit(solution)/shard_map/gather | solution.py:94
  47.9 12.6 %reduce-scatter.4.cloned.1.call-done = bf16[64,1024]{1,0:T(8,128)(2,1)} async-done(((bf16[64,8192]{1,0:T(8,128)(2,1)}), bf16[64,1024]{1,0:T(8,128)(2,1)}) %reduce-scatter.4.cloned.1.call-update) | async-done | bytes 131088 | tf_op jit(solution)/shard_map/reduce_scatter | solution.py:64
  60.5 0.0 copy-done.1
  60.5 0.9 add_convert_fusion.1
  61.4 15.6 %all_gather.7 = bf16[256,1024]{1,0:T(8,128)(2,1)S(1)} all-gather(bf16[64,1024]{1,0:T(8,128)(2,1)S(1)} %add_convert_fusion.1), channel_id=1, replica_groups=mesh['tp'=8,'grp'=4] {'grp'}, dimensions={0}, use_global_device_ids=true | all-gather | bytes 655360 | tf_op jit(solution)/shard_map/all_gather | solution.py:80
  77.0 12.2 %fusion.21 = (bf16[256,8192]{1,0:T(8,128)(2,1)}, f32[256]{0:T(256)S(1)}) fusion(s32[256]{0:T(256)S(1)} %select_reduce_fusion.2, bf16[256,1024]{1,0:T(8,128)(2,1)S(1)} %all_gather.7, bf16[1024,8192]{1,0:T(8,128)(2,1)} %param.17), kind=kOutput, calls=%fused_computation.49 | convolution fusion | flops 4303355904 | bytes 21497856 | tf_op jit(solution)/shard_map/dot_general | solution.py:79
  89.2 11.8 %psum.7 = f32[256]{0:T(256)S(1)} all-reduce(f32[256]{0:T(256)S(1)} %get-tuple-element.5), channel_id=1, replica_groups=mesh['tp'=8,'grp'=4] {'tp'}, use_global_device_ids=true, to_apply=%region_7.8 | all-reduce | flops 256 | bytes 2048 | tf_op jit(solution)/shard_map/psum | solution.py:86
  101.0 0.9 multiply_convert_fusion
  102.0 0.0 reduce-scatter.6.cloned.1.call-update
  102.0 0.0 reduce-scatter.8.cloned.1.call-start
  102.0 0.7 reduce-scatter.8.cloned.1.call-update
  102.7 21.8 %reduce-scatter.6.cloned.1.call-done = bf16[64,1024]{1,0:T(8,128)(2,1)} async-done(((bf16[256,1024]{1,0:T(8,128)(2,1)}), bf16[64,1024]{1,0:T(8,128)(2,1)}) %reduce-scatter.6.cloned.1.call-update) | async-done | bytes 131088 | tf_op jit(solution)/shard_map/reduce_scatter | solution.py:95
  124.5 1.6 add_convert_fusion
  126.1 51.4 %reduce-scatter.8.cloned.1.call-done = bf16[32,8192]{1,0:T(8,128)(2,1)} async-done(((bf16[256,8192]{1,0:T(8,128)(2,1)}), bf16[32,8192]{1,0:T(8,128)(2,1)}) %reduce-scatter.8.cloned.1.call-update) | async-done | bytes 524304 | tf_op jit(solution)/shard_map/reduce_scatter | solution.py:87
  177.5 2.0 %maximum_convert_fusion = bf16[32,8192]{1,0:T(8,128)(2,1)} fusion(bf16[32,8192]{1,0:T(8,128)(2,1)} %reduce-scatter.8.cloned.1.call-done, f32[8192]{0:T(1024)S(1)} %copy-done), kind=kLoop, calls=%fused_computation.13 | loop fusion | flops 1048576 | bytes 1081344 | tf_op jit(solution)/shard_map/convert_element_type | solution.py:90
  (13 shorter events, 0.1 us)
Async XLA Ops:
  7.2 53.3 %reduce-scatter.4.cloned.1.call-start = ((), (), s32[]{:S(2)}) async-start(), calls=%async_computation.3 | async-start | bytes 1179648 | tf_op jit(solution)/shard_map/reduce_scatter | solution.py:64
  13.2 8.4 %copy-start.2 = (s32[64,4]{0,1:T(4,128)S(1)}, s32[64,4]{0,1:T(4,128)}, u32[]{:S(2)}) copy-start(s32[64,4]{0,1:T(4,128)} %param.20) | copy-start | bytes 3076
  13.2 8.4 %copy-start.3 = (f32[64,4]{0,1:T(4,128)S(1)}, f32[64,4]{0,1:T(4,128)}, u32[]{:S(2)}) copy-start(f32[64,4]{0,1:T(4,128)} %param.21) | copy-start | bytes 3076
  13.2 23.4 %copy-start = (f32[8192]{0:T(1024)S(1)}, f32[8192]{0:T(1024)}, u32[]{:S(2)}) copy-start(f32[8192]{0:T(1024)} %param.18) | copy-start | bytes 98308
  15.6 44.9 %copy-start.1 = (bf16[64,1024]{1,0:T(8,128)(2,1)S(1)}, bf16[64,1024]{1,0:T(8,128)(2,1)}, u32[]{:S(2)}) copy-start(bf16[64,1024]{1,0:T(8,128)(2,1)} %param.11) | copy-start | bytes 393220
  21.6 102.9 %reduce-scatter.6.cloned.1.call-start = ((), (), s32[]{:S(2)}) async-start(), calls=%async_computation.4 | async-start | bytes 655360 | tf_op jit(solution)/shard_map/reduce_scatter | solution.py:95
  102.0 75.6 %reduce-scatter.8.cloned.1.call-start = ((), (), s32[]{:S(2)}) async-start(), calls=%async_computation.5 | async-start | bytes 4718592 | tf_op jit(solution)/shard_map/reduce_scatter | solution.py:87
Sparse Core Ops, SparseCore 0:
  21.7 38.7 reduce-scatter.3
  102.1 22.3 reduce-scatter.5
  127.9 49.6 reduce-scatter.7

commit v2 on v0

v2 whole, which is shorter than its diff:
```python
import functools

import jax
import jax.numpy as jnp
from jax import lax
from jax.experimental import pallas as pl
from jax.experimental.pallas import tpu as pltpu
from jax.sharding import PartitionSpec as P

HEAD_DIM = 128
KV_HEADS = 4
CHUNKS = 2
PARTS = 4
DEC_BLOCKS = 8
DEC_SLOTS = 4
TILE = 256
MESH = pl.DeviceIdType.MESH


def bits_of(count):
    found, bit = [], 1
    while bit < count:
        found.append(bit)
        bit *= 2
    return found


def flip(rank, pattern, count):
    for bit in bits_of(count):
        if pattern & bit:
            rank = rank + bit * (1 - 2 * lax.rem(lax.div(rank, bit), 2))
    return rank


def stage_plan(count, ascending):
    order = bits_of(count)
    order = order if ascending else order[:1] + order[:0:-1]
    held, stages = list(range(count)), []
    for bit in order:
        keep = [i for i, e in enumerate(held) if not e & bit]
        send = [held.index(held[i] + bit) for i in keep]
        stages.append((bit, keep, send))
        held = [held[i] for i in keep]
    return stages


def layer_kernel(
    cfg,
    ho_ref, resid_ref, table_ref, bias_ref, outw_ref, enc_ref, dec_ref,
    resid_out_ref, feat_ref,
    ho_p, outw_v, enc_v, dec_v,
    a_keep, a_send, a_recv,
    xg, xp, tg, lid_d, lid_e,
    p_keep, p_send, p_recv,
    acc, picked, pk_send, pk_recv, rows, delta, e_send, e_recv,
    outw_sem, enc_sem, dec_sem,
    a_ss, a_rs, x_ss, x_rs, t_ss, t_rs, p_ss, p_rs, k_ss, k_rs, e_ss, e_rs,
):
    tp_n, g_n, slots = cfg
    t, g = lax.axis_index("tp"), lax.axis_index("grp")
    q, _, h, width = resid_ref.shape
    lat = bias_ref.shape[1]
    span = lat // PARTS
    half = q * h
    rows_m = tp_n * h
    block = lat // DEC_BLOCKS
    own = pl.ds(g * q, q)
    tile = min(TILE, span)

    def remote(src, dst, ss, rs, axis, other):
        return pltpu.make_async_remote_copy(
            src_ref=src, dst_ref=dst, send_sem=ss, recv_sem=rs,
            device_id={axis: other}, device_id_type=MESH,
        )

    order_e = [e for e in range(tp_n) if e & 1] + [e for e in range(tp_n) if not e & 1]

    def outw_copy(e):
        cols = pl.ds(pl.multiple_of(flip(t, e, tp_n) * width, width), width)
        return pltpu.make_async_copy(outw_ref.at[:, cols], outw_v.at[e], outw_sem.at[e])

    def enc_copy(c):
        return pltpu.make_async_copy(
            enc_ref.at[:, pl.ds(c * span, span)], enc_v.at[c], enc_sem.at[c]
        )

    def dec_copy(b):
        return pltpu.make_async_copy(
            dec_ref.at[pl.ds(b * block, block)], dec_v.at[b % DEC_SLOTS], dec_sem.at[b]
        )

    for e in order_e:
        outw_copy(e).start()

    barrier = pltpu.get_barrier_semaphore()
    for e in range(1, tp_n):
        pl.semaphore_signal(
            barrier, inc=1, device_id={"tp": flip(t, e, tp_n)}, device_id_type=MESH
        )
    for e in range(1, g_n):
        pl.semaphore_signal(
            barrier, inc=1, device_id={"grp": flip(g, e, g_n)}, device_id_type=MESH
        )
    for j in range(CHUNKS):
        ho_p[j] = ho_ref[:, j].reshape(half, ho_ref.shape[3])
    tg[own] = table_ref[...]
    pl.semaphore_wait(barrier, tp_n + g_n - 2)

    table_copies = []
    for e in range(1, g_n):
        copy = remote(
            table_ref, tg.at[own], t_ss.at[e], t_rs.at[e], "grp", flip(g, e, g_n)
        )
        copy.start()
        table_copies.append(copy)

    plans = [stage_plan(tp_n, True), stage_plan(tp_n, False)]
    n_stage = len(plans[0])

    def a_copy(j, k):
        bit = plans[j % 2][k][0]
        count = tp_n >> (k + 1)
        first = tp_n - 2 * count
        part = pl.ds(first, count)
        return remote(
            a_send.at[j, part], a_recv.at[j, part], a_ss.at[j, k], a_rs.at[j, k],
            "tp", flip(t, bit, tp_n),
        )

    for place, e in enumerate(order_e):
        outw_copy(e).wait()
        part = jnp.dot(
            ho_p[...].reshape(CHUNKS * half, ho_p.shape[2]), outw_v[e],
            preferred_element_type=jnp.float32,
        )
        for j in range(CHUNKS):
            mine = part[j * half : (j + 1) * half]
            if e & 1:
                a_send[j, e >> 1] = mine.astype(jnp.bfloat16)
            else:
                a_keep[j, e >> 1] = mine
        if place == tp_n // 2 - 1:
            for j in range(CHUNKS):
                a_copy(j, 0).start()
    for c in range(PARTS):
        enc_copy(c).start()
    for b in range(DEC_SLOTS):
        dec_copy(b).start()

    def held_at(plan, k):
        held = list(range(tp_n // 2))
        for _, stay, _ in plan[1 : k + 1]:
            held = [held[s] for s in stay]
        return held

    def fold(keep, send, recv, copy, plan, j, k):
        copy(j, k - 1).wait()
        count = tp_n >> k
        first = tp_n - 2 * count
        held = held_at(plan, k - 1)
        for i, slot in enumerate(held):
            keep[j, slot] = keep[j, slot] + recv[j, first + i].astype(jnp.float32)
        if k < n_stage:
            go = plan[k][2]
            nxt = tp_n - 2 * (count // 2)
            for i, s in enumerate(go):
                send[j, nxt + i] = keep[j, held[s]].astype(jnp.bfloat16)
            copy(j, k).start()

    for k in range(1, n_stage + 1):
        for j in range(CHUNKS):
            fold(a_keep, a_send, a_recv, a_copy, plans[j % 2], j, k)

    x_copies = [[], []]
    for j in range(CHUNKS):
        mid = resid_ref[:, j].astype(jnp.float32) + a_keep[j, 0].reshape(q, h, width)
        xg[j, own] = mid.astype(jnp.bfloat16)
        for e in range(1, g_n):
            copy = remote(
                xg.at[j, own], xg.at[j, own], x_ss.at[j, e], x_rs.at[j, e],
                "grp", flip(g, e, g_n),
            )
            copy.start()
            x_copies[j].append(copy)

    for copy in table_copies:
        copy.wait()
    low = (g * lat).astype(jnp.float32)
    for j in range(CHUNKS):
        found = tg[:, j].reshape(rows_m, 128)
        local = jnp.full((rows_m, 1), -1.0, jnp.float32)
        value = jnp.zeros((rows_m, 1), jnp.float32)
        for c in range(slots):
            place = found[:, c : c + 1] - low
            inside = (place >= 0.0) & (place < float(lat))
            local = jnp.where(inside, place, local)
            value = jnp.where(inside, found[:, slots + c : slots + c + 1], value)
        wide = jnp.broadcast_to(local, (rows_m, 128)).astype(jnp.int32)
        lid_d[j] = wide.reshape(tp_n, h, 128)
        delta[j] = jnp.broadcast_to(value, (rows_m, 128)).reshape(tp_n, h, 128)
    for j in range(CHUNKS):
        for e in range(tp_n):
            lid_e[j, e] = lid_d[j, flip(t, e, tp_n)]
    acc[...] = jnp.zeros_like(acc)
    rows[...] = jnp.zeros_like(rows)

    def dec_step(b):
        dec_copy(b).wait()
        lane = lax.broadcasted_iota(jnp.int32, (CHUNKS * rows_m, 128), 1)
        local = lid_d[...].reshape(CHUNKS * rows_m, 128)
        pieces = [
            jnp.where(local == lane + (b * block + n), 1.0, 0.0).astype(jnp.bfloat16)
            for n in range(0, block, 128)
        ]
        hot = jnp.concatenate(pieces, axis=1)
        got = jnp.dot(hot, dec_v[b % DEC_SLOTS], preferred_element_type=jnp.float32)
        rows[...] += got.reshape(rows.shape)
        if b + DEC_SLOTS < DEC_BLOCKS:
            dec_copy(b + DEC_SLOTS).start()

    for b in range(DEC_SLOTS):
        dec_step(b)

    pieces = CHUNKS * PARTS
    bias_on = jnp.where(t == 0, 1.0, 0.0).astype(jnp.float32)

    def p_copy(p, k):
        bit = plans[p % 2][k][0]
        count = tp_n >> (k + 1)
        part = pl.ds(tp_n - 2 * count, count)
        return remote(
            p_send.at[p, part], p_recv.at[p, part], p_ss.at[p, k], p_rs.at[p, k],
            "tp", flip(t, bit, tp_n),
        )

    def multiply(p):
        j, c = p // PARTS, p % PARTS
        if c == 0:
            for copy in x_copies[j]:
                copy.wait()
            for e in range(tp_n):
                xp[j, e] = xg[j, flip(t, e, tp_n)]
        if j == 0:
            enc_copy(c).wait()

        def body(n, _):
            cols = pl.ds(pl.multiple_of(n * tile, tile), tile)
            part = jnp.dot(
                xp[j].reshape(rows_m, width), enc_v[c, :, cols],
                preferred_element_type=jnp.float32,
            )
            lane = lax.broadcasted_iota(jnp.int32, (rows_m, 128), 1)
            local = lid_e[j].reshape(rows_m, 128)
            total = acc[j].reshape(rows_m, 128)
            for m in range(0, tile, 128):
                at = pl.multiple_of(c * span + n * tile + m, 128)
                shift = bias_ref[:, pl.ds(at, 128)] * bias_on
                total = total + jnp.where(
                    local == lane + at, part[:, m : m + 128] + shift, 0.0
                )
            acc[j] = total.reshape(tp_n, h, 128)
            for e in range(tp_n):
                rows_e = part[e * h : (e + 1) * h]
                if e & 1:
                    p_send[p, e >> 1, :, cols] = rows_e.astype(jnp.bfloat16)
                else:
                    p_keep[p, e >> 1, :, cols] = rows_e
            return 0

        lax.fori_loop(0, span // tile, body, 0)
        p_copy(p, 0).start()

    def finish(p):
        j, c = p // PARTS, p % PARTS
        cols = pl.ds(c * span, span)
        whole = p_keep[p, 0] + bias_ref[:, cols]
        feat_ref[pl.ds(j * h, h), cols] = jnp.maximum(whole, 0.0).astype(jnp.bfloat16)

    eye = lax.broadcasted_iota(jnp.int32, (rows_m, rows_m), 0) == lax.broadcasted_iota(
        jnp.int32, (rows_m, rows_m), 1
    )

    def pick_copy(j, e):
        return remote(
            pk_send.at[j], pk_recv.at[j, e], k_ss.at[j, e], k_rs.at[j, e],
            "tp", flip(t, e, tp_n),
        )

    def pick(j):
        for e in range(tp_n):
            picked[j, flip(t, e, tp_n)] = acc[j, e]
        column = jnp.sum(picked[j].reshape(rows_m, 128), axis=1, keepdims=True)
        line = jnp.sum(jnp.where(eye, column, 0.0), axis=0, keepdims=True)
        pk_send[j] = jnp.broadcast_to(line, (8, rows_m))
        for e in range(1, tp_n):
            pick_copy(j, e).start()

    def edit_copy(j, e):
        return remote(
            e_send.at[j, e], e_recv.at[j, e], e_ss.at[j, e], e_rs.at[j, e],
            "grp", flip(g, e, g_n),
        )

    def edit(j):
        line = pk_send[j]
        for e in range(1, tp_n):
            pick_copy(j, e).wait()
            line = line + pk_recv[j, e]
        column = jnp.sum(jnp.where(eye, line[:1], 0.0), axis=1, keepdims=True)
        now = jnp.maximum(column, 0.0).astype(jnp.bfloat16).astype(jnp.float32)
        change = delta[j].reshape(rows_m, 128)[:, :1] - now
        change = change.astype(jnp.bfloat16).astype(jnp.float32)
        delta[j] = jnp.broadcast_to(change, (rows_m, 128)).reshape(tp_n, h, 128)
        for e in range(1, g_n):
            there = pl.ds(flip(g, e, g_n) * q, q)
            step = delta[j, there]
            e_send[j, e] = (rows[j, there] * step[:, :, :1]).astype(jnp.bfloat16)
            edit_copy(j, e).start()

    def close(j):
        total = xg[j, own].astype(jnp.float32)
        edits = rows[j, own] * delta[j, own][:, :, :1]
        for e in range(1, g_n):
            edit_copy(j, e).wait()
            edits = edits + e_recv[j, e].astype(jnp.float32)
        resid_out_ref[:, j] = (total + edits).astype(jnp.bfloat16)

    for s in range(pieces + n_stage):
        if s < pieces:
            multiply(s)
            if s % PARTS == PARTS - 1:
                pick(s // PARTS)
        for k in range(n_stage, 0, -1):
            p = s - k
            if 0 <= p < pieces:
                fold(p_keep, p_send, p_recv, p_copy, plans[p % 2], p, k)
                if k == n_stage:
                    finish(p)
        if s < DEC_BLOCKS - DEC_SLOTS:
            dec_step(s + DEC_SLOTS)
        if s == PARTS:
            edit(0)
        if s == pieces:
            edit(1)
    for j in range(CHUNKS):
        close(j)


def layer(ho, resid_in, table, enc_bias, out_weight, enc_weight, dec_weight, slots):
    tp_n, g_n = lax.axis_size("tp"), lax.axis_size("grp")
    rc, width = resid_in.shape
    depth = ho.shape[1]
    lat = enc_weight.shape[1]
    out_rows = rc * g_n // tp_n
    q, h = rc // out_rows, out_rows // CHUNKS
    half = q * h
    span, block = lat // PARTS, lat // DEC_BLOCKS
    pieces = CHUNKS * PARTS
    n_stage = len(bits_of(tp_n))
    bf16, f32 = jnp.bfloat16, jnp.float32
    vmem = pl.BlockSpec(memory_space=pltpu.VMEM)
    hbm = pl.BlockSpec(memory_space=pl.ANY)
    dma = pltpu.SemaphoreType.DMA
    resid_out, feat = pl.pallas_call(
        functools.partial(layer_kernel, (tp_n, g_n, slots)),
        out_shape=(
            jax.ShapeDtypeStruct((q, CHUNKS, h, width), bf16),
            jax.ShapeDtypeStruct((out_rows, lat), bf16),
        ),
        in_specs=[vmem, vmem, vmem, vmem, hbm, hbm, hbm],
        out_specs=(vmem, vmem),
        scratch_shapes=[
            pltpu.VMEM((CHUNKS, half, depth), bf16),
            pltpu.VMEM((tp_n, depth, width), bf16),
            pltpu.VMEM((PARTS, width, span), bf16),
            pltpu.VMEM((DEC_SLOTS, block, width), bf16),
            pltpu.VMEM((CHUNKS, tp_n // 2, half, width), f32),
            pltpu.VMEM((CHUNKS, tp_n - 1, half, width), bf16),
            pltpu.VMEM((CHUNKS, tp_n - 1, half, width), bf16),
            pltpu.VMEM((CHUNKS, tp_n, h, width), bf16),
            pltpu.VMEM((CHUNKS, tp_n, h, width), bf16),
            pltpu.VMEM((tp_n, CHUNKS, h, 128), f32),
            pltpu.VMEM((CHUNKS, tp_n, h, 128), jnp.int32),
            pltpu.VMEM((CHUNKS, tp_n, h, 128), jnp.int32),
            pltpu.VMEM((pieces, tp_n // 2, h, span), f32),
            pltpu.VMEM((pieces, tp_n - 1, h, span), bf16),
            pltpu.VMEM((pieces, tp_n - 1, h, span), bf16),
            pltpu.VMEM((CHUNKS, tp_n, h, 128), f32),
            pltpu.VMEM((CHUNKS, tp_n, h, 128), f32),
            pltpu.VMEM((CHUNKS, 8, tp_n * h), f32),
            pltpu.VMEM((CHUNKS, tp_n, 8, tp_n * h), f32),
            pltpu.VMEM((CHUNKS, tp_n, h, width), f32),
            pltpu.VMEM((CHUNKS, tp_n, h, 128), f32),
            pltpu.VMEM((CHUNKS, g_n, q, h, width), bf16),
            pltpu.VMEM((CHUNKS, g_n, q, h, width), bf16),
            dma((tp_n,)), dma((PARTS,)), dma((DEC_BLOCKS,)),
            dma((CHUNKS, n_stage)), dma((CHUNKS, n_stage)),
            dma((CHUNKS, g_n)), dma((CHUNKS, g_n)),
            dma((g_n,)), dma((g_n,)),
            dma((pieces, n_stage)), dma((pieces, n_stage)),
            dma((CHUNKS, tp_n)), dma((CHUNKS, tp_n)),
            dma((CHUNKS, g_n)), dma((CHUNKS, g_n)),
        ],
        compiler_params=pltpu.CompilerParams(
            collective_id=0, has_side_effects=True, vmem_limit_bytes=60 * 2**20
        ),
    )(
        ho.reshape(q, CHUNKS, h, depth),
        resid_in.reshape(q, CHUNKS, h, width),
        table.reshape(q, CHUNKS, h, 128),
        enc_bias.reshape(1, lat),
        out_weight, enc_weight, dec_weight,
    )
    return resid_out.reshape(rc, width), feat


def per_device(
    resid_in,
    queries,
    kv_cache,
    new_kv,
    lengths,
    out_weight,
    enc_weight,
    enc_bias,
    dec_weight,
    clamp_ids,
    clamp_values,
):
    tp_count = lax.axis_size("tp")
    tp_rank = lax.axis_index("tp")
    row_count = resid_in.shape[0]
    own_heads = queries.shape[1] // HEAD_DIM
    slot_count = kv_cache.shape[3]
    score_scale = HEAD_DIM ** (-0.5)
    query_heads = queries.reshape(row_count, own_heads, HEAD_DIM)
    cache_keys = kv_cache[0, :, 0]
    cache_values = kv_cache[1, :, 0]
    kv_index = tp_rank // (tp_count // KV_HEADS)
    new_key = lax.dynamic_index_in_dim(new_kv[0], kv_index, 1, keepdims=False)
    new_value = lax.dynamic_index_in_dim(new_kv[1], kv_index, 1, keepdims=False)
    scores = (
        jnp.einsum("shd,spd->shp", query_heads, cache_keys, preferred_element_type=jnp.float32)
        * score_scale
    )
    new_score = (
        jnp.einsum("shd,sd->sh", query_heads, new_key, preferred_element_type=jnp.float32)
        * score_scale
    )
    slot_index = jnp.arange(slot_count, dtype=jnp.int32)
    is_valid = (slot_index[None, :] < lengths[:, None])[:, None, :]
    top_score = jnp.maximum(jnp.max(jnp.where(is_valid, scores, -jnp.inf), axis=-1), new_score)
    prob_cache = jnp.where(is_valid, jnp.exp(scores - top_score[..., None]), 0.0)
    new_prob = jnp.exp(new_score - top_score)
    total_weight = jnp.sum(prob_cache, axis=-1) + new_prob
    new_rounded = lax.optimization_barrier(new_prob.astype(jnp.bfloat16)).astype(jnp.float32)
    weighted = jnp.einsum(
        "shp,spd->shd",
        prob_cache.astype(jnp.bfloat16),
        cache_values,
        preferred_element_type=jnp.float32,
    )
    weighted = weighted + new_rounded[..., None] * new_value.astype(jnp.float32)[:, None, :]
    head_output = (
        (weighted / total_weight[..., None])
        .astype(jnp.bfloat16)
        .reshape(row_count, own_heads * HEAD_DIM)
    )
    slots = clamp_ids.shape[1]
    table = jnp.concatenate(
        [
            clamp_ids.astype(jnp.float32),
            clamp_values,
            jnp.zeros((row_count, 128 - 2 * slots), jnp.float32),
        ],
        axis=1,
    )
    resid_out, feature_out = layer(
        head_output, resid_in, table, enc_bias, out_weight, enc_weight, dec_weight, slots
    )
    return (resid_out, feature_out)


def solution(mesh):
    placed = (
        P("grp", "tp"),
        P("grp", "tp"),
        P(None, "grp", "tp", None, None),
        P(None, "grp", None, None),
        P("grp"),
        P("tp", None),
        P("tp", "grp"),
        P("grp"),
        P("grp", "tp"),
        P("grp", None),
        P("grp", None),
    )
    return jax.shard_map(
        per_device,
        mesh=mesh,
        in_specs=placed,
        out_specs=(P("grp", "tp"), P("tp", "grp")),
        check_vma=False,
    )
```

time: 307 us -> 89.8 us (0.29)
  waiting for transfers between devices: 197 us -> 0 us
  Pallas kernels: 0 us -> 72.9 us
  blocking collectives: 39.9 us -> 0 us
  matrix products: 38.1 us -> 5.39 us
  between operations: 13.8 us -> 0.72 us
  other arithmetic: 13 us -> 2.44 us
    psum x2 -> x0, waiting for transfers between devices: 153 us -> none  [the longest x1 102 us: per_device(): pre_act = lax.psum(pre_part, 'tp')]
    pallas_call x0 -> x1, Pallas kernels: none -> 72.9 us  [layer(): pl.pallas_call(functools.partial(layer_kernel, (tp_n, g_n, slots)), out_s...]
    reduce_scatter x1 -> x0, waiting for transfers between devices: 44 us -> none  [per_device(): lax.psum_scatter(attn_part, 'tp', scatter_dimension=1, tiled=True)]
    all_gather x3 -> x0, blocking collectives: 39.9 us -> none  [the longest x1 15.6 us: per_device(): lax.all_gather(resid_mid, 'grp', axis=0, tiled=True)]
    dot_general x3 -> x0, matrix products: 32.8 us -> none  [the longest x1 14 us: per_device(): jnp.dot(delta_lat, dec_weight, preferred_element_type=jnp.float32)]
    reduce_sum x1 -> x0, other arithmetic: 9.31 us -> none  [clamp_delta(): jnp.sum(jnp.where(is_hit, current, 0.0), axis=1, keepdims=True)]
    unnamed x10 -> x4, local copies, waits for them, and re-layouts: 0.7 us -> 4.21 us
  transfers between devices with their start and end apart: 3 -> 0, of which waited for: 3 -> 0; matrix products, arithmetic and copies ran while one was open for 1% -> 0% of each run, Pallas kernels for 0% -> 0%
where the time goes in v2:
time: 89.8 us; the launch traced here: 88.2 us
  Pallas kernels  72.9 us (81%)
  local copies, waits for them, and re-layouts  6.83 us (8%)
  matrix products  5.39 us (6%)
  other arithmetic  2.44 us (3%)
    pallas_call x1, Pallas kernels, layer(): pl.pallas_call(functools.partial(layer_kernel, (tp_n, g_n, slots)), out_s...  72.9 us
    unnamed x4, local copies, waits for them, and re-layouts  4.21 us
    dot_general x1, matrix products, per_device(): jnp.einsum('shd,spd->shp', query_heads, cache_keys, preferred_element_typ...  2.87 us
    dot_general x1, matrix products, per_device(): jnp.einsum('shp,spd->shd', prob_cache.astype(jnp.bfloat16), cache_values,...  2.32 us

profile of v2, /device:TPU:0, one launch (start us, length us, event | category | flops | bytes accessed | tf_op | source)
XLA Modules:
  0.0 88.2 jit_solution(6858188969082840837)
XLA Ops:
  0.7 0.1 pad.2.clone
  0.7 0.7 convert_element_type.31
  1.4 0.7 iota_compare_fusion
  2.2 0.1 copy.20
  2.2 0.8 copy.21
  3.0 0.7 maximum_maximum_fusion
  3.7 0.9 reshape.50
  4.6 0.9 %fusion.17 = (bf16[1,64,4,128]{3,2,1,0:T(4,128)(2,1)S(1)}, bf16[1,64,4,128]{3,2,1,0:T(4,128)(2,1)S(1)}) fusion(bf16[2,64,4,128]{3,2,1,0:T(4,128)(2,1)} %param.14), kind=kLoop, calls=%fused_computation.27 | loop fusion | bytes 262144 | tf_op jit(solution)/shard_map/slice | solution.py:441
  5.5 0.1 dynamic-slice_convert_fusion
  5.6 0.2 fusion.12
  5.8 2.9 %select_reduce_fusion = (f32[64,4]{1,0:T(8,128)S(1)}, f32[64,4,128]{2,1,0:T(4,128)S(1)}) fusion(pred[64,128]{1,0:T(8,128)(4,1)S(1)} %iota_compare_fusion, bf16[64,4,128]{2,1,0:T(4,128)(2,1)S(1)} %reshape.50, bf16[2,64,1,128,128]{4,3,1,2,0:T(8,128)(2,1)} %bitcast.40), kind=kOutput, calls=%fused_computation.9 | convolution fusion | flops 8486656 | bytes 2302976 | tf_op jit(solution)/shard_map/shd,spd->shp/dot_general | solution.py:443
  8.7 0.2 fusion.6
  8.9 2.3 %fusion.5 = bf16[64,4,128]{2,1,0:T(4,128)(2,1)S(1)} fusion(bf16[2,64,1,128,128]{4,3,1,2,0:T(8,128)(2,1)} %bitcast.41, f32[64,4,128]{2,1,0:T(4,128)S(1)} %get-tuple-element.11, f32[64,4]{1,0:T(8,128)S(1)} %get-tuple-element.9, f32[64,128]{1,0:T(8,128)S(1)} %bitcast.38, f32[64,4]{1,0:T(8,128)S(1)} %convert_element_type.27, ...), kind=kOutput, calls=%fused_computation.7 | convolution fusion | flops 8617984 | bytes 2337792 | tf_op jit(solution)/shard_map/shp,spd->shd/dot_general | solution.py:457
  11.3 0.7 reshape_reshape.3.ho_ref
  11.9 72.9 %shard_map.122 = (bf16[2,2,16,1024]{3,2,1,0:T(8,128)(2,1)}, bf16[32,8192]{1,0:T(8,128)(2,1)}) custom-call(bf16[2,2,16,512]{3,2,1,0:T(8,128)(2,1)} %reshape_reshape.3.ho_ref, bf16[2,2,16,1024]{3,2,1,0:T(8,128)(2,1)} %bitcast.32, f32[2,2,16,128]{3,2,1,0:T(8,128)} %bitcast.33, f32[1,8192]{1,0:T(1,128)} %bitcast.37, bf16[512,8192]{1,0:T(8,128)(2,1)} %outw_ref.1, ...), custom_call_target="tpu_custom_call" | custom-call | tf_op jit(solution)/shard_map/pallas_call | solution.py:364
  84.8 1.6 %copy.32 = bf16[64,1024]{1,0:T(8,128)(2,1)} copy(bf16[64,1024]{1,0:T(8,128)(2,1)} %bitcast.34) | data formatting | bytes 262144
  86.4 1.9 %copy.33 = bf16[32,8192]{1,0:T(8,128)(2,1)} copy(bf16[32,8192]{1,0:T(8,128)(2,1)} %get-tuple-element.17) | data formatting | bytes 1048576
  (5 shorter events, 0.0 us)

commit v3 on v2

--- a/solution.py
+++ b/solution.py
@@ -325,23 +325,23 @@
             edits = edits + e_recv[j, e].astype(jnp.float32)
         resid_out_ref[:, j] = (total + edits).astype(jnp.bfloat16)
 
-    for s in range(pieces + n_stage):
+    for s in range(pieces + 2 * n_stage - 1):
         if s < pieces:
             multiply(s)
             if s % PARTS == PARTS - 1:
                 pick(s // PARTS)
-        for k in range(n_stage, 0, -1):
-            p = s - k
+        for k in range(1, n_stage + 1):
+            p = s - 2 * k + 1
             if 0 <= p < pieces:
                 fold(p_keep, p_send, p_recv, p_copy, plans[p % 2], p, k)
                 if k == n_stage:
                     finish(p)
+            if k == 1 and s == PARTS:
+                edit(0)
+            if k == 1 and s == pieces:
+                edit(1)
         if s < DEC_BLOCKS - DEC_SLOTS:
             dec_step(s + DEC_SLOTS)
-        if s == PARTS:
-            edit(0)
-        if s == pieces:
-            edit(1)
     for j in range(CHUNKS):
         close(j)
 

time: 89.8 us -> 76.7 us (0.85); the launches traced: 88.2 us -> 76.2 us
  Pallas kernels: 72.9 us -> 60.9 us
    pallas_call x1, Pallas kernels: 72.9 us -> 60.9 us  [layer(): pl.pallas_call(functools.partial(layer_kernel, (tp_n, g_n, slots)), out_s...]
where the time goes in v3:
time: 76.7 us; the launch traced here: 76.2 us
  Pallas kernels  60.9 us (79%)
  local copies, waits for them, and re-layouts  6.83 us (9%)
  matrix products  5.39 us (7%)
  other arithmetic  2.44 us (3%)
    pallas_call x1, Pallas kernels, layer(): pl.pallas_call(functools.partial(layer_kernel, (tp_n, g_n, slots)), out_s...  60.9 us
    unnamed x4, local copies, waits for them, and re-layouts  4.21 us
    dot_general x1, matrix products, per_device(): jnp.einsum('shd,spd->shp', query_heads, cache_keys, preferred_element_typ...  2.87 us
    dot_general x1, matrix products, per_device(): jnp.einsum('shp,spd->shd', prob_cache.astype(jnp.bfloat16), cache_values,...  2.32 us

profile of v3, /device:TPU:0, one launch (start us, length us, event | category | flops | bytes accessed | tf_op | source)
XLA Modules:
  0.0 76.2 jit_solution(5994140103062263307)
XLA Ops:
  0.7 0.1 pad.2.clone
  0.7 0.7 convert_element_type.31
  1.4 0.7 iota_compare_fusion
  2.2 0.1 copy.20
  2.2 0.8 %copy.21 = f32[64,4]{1,0:T(8,128)S(1)} copy(f32[64,4]{0,1:T(4,128)} %param.21) | data formatting | bytes 2048 | tf_op args[10]
  3.0 0.7 maximum_maximum_fusion
  3.7 0.9 %reshape.50 = bf16[64,4,128]{2,1,0:T(4,128)(2,1)S(1)} reshape(bf16[64,512]{1,0:T(8,128)(2,1)} %param.12) | data formatting | bytes 131072 | tf_op jit(solution)/shard_map/reshape | solution.py:436
  4.6 0.9 %fusion.17 = (bf16[1,64,4,128]{3,2,1,0:T(4,128)(2,1)S(1)}, bf16[1,64,4,128]{3,2,1,0:T(4,128)(2,1)S(1)}) fusion(bf16[2,64,4,128]{3,2,1,0:T(4,128)(2,1)} %param.14), kind=kLoop, calls=%fused_computation.27 | loop fusion | bytes 262144 | tf_op jit(solution)/shard_map/slice | solution.py:441
  5.5 0.1 dynamic-slice_convert_fusion
  5.6 0.2 fusion.12
  5.8 2.9 %select_reduce_fusion = (f32[64,4]{1,0:T(8,128)S(1)}, f32[64,4,128]{2,1,0:T(4,128)S(1)}) fusion(pred[64,128]{1,0:T(8,128)(4,1)S(1)} %iota_compare_fusion, bf16[64,4,128]{2,1,0:T(4,128)(2,1)S(1)} %reshape.50, bf16[2,64,1,128,128]{4,3,1,2,0:T(8,128)(2,1)} %bitcast.40), kind=kOutput, calls=%fused_computation.9 | convolution fusion | flops 8486656 | bytes 2302976 | tf_op jit(solution)/shard_map/shd,spd->shp/dot_general | solution.py:443
  8.7 0.2 fusion.6
  8.9 2.3 %fusion.5 = bf16[64,4,128]{2,1,0:T(4,128)(2,1)S(1)} fusion(bf16[2,64,1,128,128]{4,3,1,2,0:T(8,128)(2,1)} %bitcast.41, f32[64,4,128]{2,1,0:T(4,128)S(1)} %get-tuple-element.11, f32[64,4]{1,0:T(8,128)S(1)} %get-tuple-element.9, f32[64,128]{1,0:T(8,128)S(1)} %bitcast.38, f32[64,4]{1,0:T(8,128)S(1)} %convert_element_type.27, ...), kind=kOutput, calls=%fused_computation.7 | convolution fusion | flops 8617984 | bytes 2337792 | tf_op jit(solution)/shard_map/shp,spd->shd/dot_general | solution.py:457
  11.3 0.7 reshape_reshape.3.ho_ref
  11.9 60.9 %shard_map.122 = (bf16[2,2,16,1024]{3,2,1,0:T(8,128)(2,1)}, bf16[32,8192]{1,0:T(8,128)(2,1)}) custom-call(bf16[2,2,16,512]{3,2,1,0:T(8,128)(2,1)} %reshape_reshape.3.ho_ref, bf16[2,2,16,1024]{3,2,1,0:T(8,128)(2,1)} %bitcast.32, f32[2,2,16,128]{3,2,1,0:T(8,128)} %bitcast.33, f32[1,8192]{1,0:T(1,128)} %bitcast.37, bf16[512,8192]{1,0:T(8,128)(2,1)} %outw_ref.1, ...), custom_call_target="tpu_custom_call" | custom-call | tf_op jit(solution)/shard_map/pallas_call | solution.py:364
  72.8 1.6 %copy.32 = bf16[64,1024]{1,0:T(8,128)(2,1)} copy(bf16[64,1024]{1,0:T(8,128)(2,1)} %bitcast.34) | data formatting | bytes 262144
  74.4 1.9 %copy.33 = bf16[32,8192]{1,0:T(8,128)(2,1)} copy(bf16[32,8192]{1,0:T(8,128)(2,1)} %get-tuple-element.17) | data formatting | bytes 1048576
  (5 shorter events, 0.0 us)
